TPU v7x, 256 devices: a whole 4x4x8 slice. The times are simulated.
256 devices in a mesh: segment: 4 (over z_hi), mp: 16 (over y, x), dp: 4 (over z_lo, core).
Axes of the slice: x: 4, y: 4, z: 8 (z_hi: 4, z_lo: 2; z = z_hi * 2 + z_lo), core: 2. Of those that a mesh axis runs over, the one named last changes fastest.
Arguments:
- frames: bfloat16 [128, 128, 1536], P(('segment', 'dp'), 'mp'), may hold values from -6 to 6
- latent_init: bfloat16 [64, 1536], replicated, may hold values from -6 to 6
- norm_gains: bfloat16 [3, 1536], replicated, may hold values from 0.099609375 to 1.8984375
- res_query: bfloat16 [1536, 1536], P(None, 'mp'), may hold values from -0.15625 to 0.15625
- res_kv: bfloat16 [1536, 2, 1536], P(None, None, 'mp'), may hold values from -0.15625 to 0.15625
- res_out: bfloat16 [1536, 1536], replicated, may hold values from -0.15625 to 0.15625
- text: bfloat16 [4, 4, 768, 8192], P('segment', 'dp', None, 'mp'), may hold values from -6 to 6
- text_gain: bfloat16 [4, 8192], P('segment'), may hold values from 0.099609375 to 1.8984375
- w_query: bfloat16 [4, 8192, 8192], P('segment', 'dp', 'mp'), may hold values from -0.0625 to 0.0625
- w_kv: bfloat16 [4, 1536, 2, 8192], P('segment', 'dp', None, 'mp'), may hold values from -0.15625 to 0.15625
- xgate: float32 [4], P('segment'), may hold values from 0.3 to 1.2
- frame_counts: int32 [4, 4], P('segment', 'dp'), may hold values from 1 to 8
- frame_dest: int32 [128], replicated, may hold values from 0 to 127, each once
- cotangent: bfloat16 [4, 4, 768, 8192], P('segment', 'dp', None, 'mp'), may hold values from -6 to 6
Outputs:
- context: bfloat16 [4, 4, 768, 8192], P('segment', 'dp', None, 'mp')
- latent_grad: float32 [64, 128, 1536], P('mp', ('segment', 'dp'))
Inputs may be any that keep to these rules, and one draw needn't show every extreme that they name: frame_dest is a permutation of the slots; a slot is used by its destination sequence only if its frame number is below that sequence's frame count.
All inputs are finite; a program needn't handle non-finite values.
Results may differ from a plain program's by a relative error of at most 0.04.
Values may be sent and summed in bfloat16 or wider, within the bound.
No kernel may reach another device: no remote copies, remote signals or barrier semaphores. Data moves between devices by JAX's collectives and lax.ppermute only.
A program may use at most 128 MiB of HBM per device.

v0:
```python
import math
import jax
import jax.numpy as jnp
from jax import lax
from jax.sharding import PartitionSpec as P

HD = 128
E = 1536
RESAMPLE_HEAD_DIM = 96
LAT = 64
FMAX = 8


def layer_norm(inputs, gain_row):
    values = inputs.astype(jnp.float32)
    center = values - jnp.mean(values, axis=-1, keepdims=True)
    spread = jnp.mean(center * center, axis=-1, keepdims=True)
    return center * lax.rsqrt(spread + 1e-05) * gain_row.astype(jnp.float32)


def attend(query_matrix, key_value_block, live, gate):
    score_matrix = jnp.einsum(
        "rag,lag->arl", query_matrix, key_value_block[:, 0], preferred_element_type=jnp.float32
    ) / math.sqrt(query_matrix.shape[-1])
    score_matrix = jnp.where(live[None, None, :], score_matrix, -1e30)
    row_max = lax.stop_gradient(jnp.max(score_matrix, axis=-1, keepdims=True))
    unnormalized_weights = jnp.exp(score_matrix - row_max)
    row_sum = jnp.sum(unnormalized_weights, axis=-1)
    blended_values = jnp.einsum(
        "lfv,vla->fla",
        unnormalized_weights.astype(jnp.bfloat16),
        key_value_block[:, 1],
        preferred_element_type=jnp.float32,
    )
    blended_values = blended_values / jnp.transpose(row_sum)[:, :, None]
    return gate * blended_values.reshape(blended_values.shape[0], -1)


def per_device(
    frames,
    latent_init,
    norm_gains,
    res_query,
    res_kv,
    res_out,
    text,
    text_gain,
    w_query,
    w_kv,
    xgate,
    frame_counts,
    frame_dest,
    cotangent,
):
    mp_count = lax.axis_size("mp")
    share = LAT // mp_count
    slots = frame_dest.shape[0]
    owned = frames.shape[0]
    res_cols = res_query.shape[1]
    res_local = res_cols // RESAMPLE_HEAD_DIM
    res_scale = 1.0 / math.sqrt(RESAMPLE_HEAD_DIM)
    lat_norm = layer_norm(latent_init, norm_gains[1]).astype(jnp.bfloat16)
    resampler_heads = (
        jnp.dot(lat_norm, res_query, preferred_element_type=jnp.float32)
        .astype(jnp.bfloat16)
        .reshape(LAT, res_local, RESAMPLE_HEAD_DIM)
    )
    latent_pair_rows = (
        jnp.einsum("le,ekc->lkc", lat_norm, res_kv, preferred_element_type=jnp.float32)
        .astype(jnp.bfloat16)
        .reshape(LAT, 2, res_local, RESAMPLE_HEAD_DIM)
    )
    first_scores = (
        jnp.einsum(
            "epg,apg->pea",
            resampler_heads,
            latent_pair_rows[:, 0],
            preferred_element_type=jnp.float32,
        )
        * res_scale
    )
    first_max = jnp.max(first_scores, axis=-1)
    first_exp = jnp.exp(first_scores - first_max[:, :, None])
    first_sum = jnp.sum(first_exp, axis=-1)
    first_acc = jnp.einsum(
        "nvf,fnr->nvr",
        first_exp.astype(jnp.bfloat16),
        latent_pair_rows[:, 1],
        preferred_element_type=jnp.float32,
    )
    piece = lax.all_gather(frames, "mp", axis=1, tiled=True)
    run_max = jnp.broadcast_to(first_max, (owned,) + first_max.shape)
    run_sum = jnp.broadcast_to(first_sum, (owned,) + first_sum.shape)
    run_acc = jnp.broadcast_to(first_acc, (owned,) + first_acc.shape)
    width = piece.shape[1]
    media = layer_norm(piece, norm_gains[0]).astype(jnp.bfloat16)
    media_pairs = (
        jnp.einsum("fpe,ekc->fpkc", media, res_kv, preferred_element_type=jnp.float32)
        .astype(jnp.bfloat16)
        .reshape(owned, width, 2, res_local, RESAMPLE_HEAD_DIM)
    )
    score_matrix = (
        jnp.einsum(
            "lhd,fphd->fhlp",
            resampler_heads,
            media_pairs[:, :, 0],
            preferred_element_type=jnp.float32,
        )
        * res_scale
    )
    new_max = jnp.maximum(run_max, jnp.max(score_matrix, axis=-1))
    fade = jnp.exp(run_max - new_max)
    unnormalized_weights = jnp.exp(score_matrix - new_max[..., None])
    new_sum = run_sum * fade + jnp.sum(unnormalized_weights, axis=-1)
    new_acc = run_acc * fade[..., None] + jnp.einsum(
        "fhlp,fphd->fhld",
        unnormalized_weights.astype(jnp.bfloat16),
        media_pairs[:, :, 1],
        preferred_element_type=jnp.float32,
    )
    res_context = (new_acc / new_sum[..., None]).astype(jnp.bfloat16)
    out_rows = lax.dynamic_slice_in_dim(res_out, lax.axis_index("mp") * res_cols, res_cols, 0)
    out_heads = out_rows.reshape(res_local, RESAMPLE_HEAD_DIM, E)
    part = res_context
    update = lax.psum_scatter(
        jnp.einsum("fhlr,hre->lfe", part, out_heads, preferred_element_type=jnp.float32).astype(
            jnp.bfloat16
        ),
        "mp",
        scatter_dimension=0,
        tiled=True,
    ).astype(jnp.float32)
    base_rows = lax.dynamic_slice_in_dim(
        latent_init, lax.axis_index("mp") * share, share, 0
    ).astype(jnp.float32)
    latents = layer_norm(base_rows[:, None, :] + update, norm_gains[2]).astype(jnp.bfloat16)
    gathered = lax.all_gather(latents, ("segment", "dp"), axis=1, tiled=True)
    group = lax.axis_index(("segment", "dp"))
    wanted = group * owned + jnp.arange(owned, dtype=jnp.int32)
    picker = (frame_dest[None, :] == wanted[:, None]).astype(jnp.bfloat16)
    mine = jnp.einsum("js,rse->rje", picker, gathered, preferred_element_type=jnp.float32).astype(
        jnp.bfloat16
    )
    dest = lax.all_gather(mine, "mp", axis=0, tiled=True)
    whole_text = lax.all_gather(text[0], "mp", axis=2, tiled=True)
    seq_local = whole_text.shape[0]
    txt_len = whole_text.shape[1]
    tokens = seq_local * txt_len
    text_norm = (
        layer_norm(whole_text, text_gain[0])
        .astype(jnp.bfloat16)
        .reshape(tokens, whole_text.shape[2])
    )
    head_cols = w_query.shape[2]
    head_local = head_cols // HD
    query_sum = jnp.dot(
        text_norm,
        lax.all_gather(w_query[0], "dp", axis=0, tiled=True),
        preferred_element_type=jnp.float32,
    )
    query_matrix = query_sum.astype(jnp.bfloat16).reshape(seq_local, txt_len, head_local, HD)
    full_kv = lax.all_gather(w_kv[0], "dp", axis=0, tiled=True)
    pair_sum = jnp.einsum("lje,ekc->jlkc", dest, full_kv, preferred_element_type=jnp.float32)
    pair_list = pair_sum.astype(jnp.bfloat16).reshape(seq_local, FMAX * LAT, 2, head_local, HD)
    live = jnp.repeat(
        jnp.arange(FMAX, dtype=jnp.int32)[None, :] < frame_counts[0][:, None], LAT, axis=1
    )
    gate = jnp.tanh(xgate[0])

    def local_attend(pair_in):
        return jax.vmap(attend, in_axes=(0, 0, 0, None))(query_matrix, pair_in, live, gate)

    gated, pull = jax.vjp(local_attend, pair_list)
    context = gated.astype(jnp.bfloat16)[None]
    (pair_grad,) = pull(cotangent[0].astype(jnp.float32))
    pair_grad = pair_grad.reshape(owned, LAT, 2, head_cols)
    part = pair_grad
    dest_grad = lax.psum_scatter(
        jnp.einsum("jlkc,ekc->lje", part, full_kv, preferred_element_type=jnp.float32).astype(
            jnp.bfloat16
        ),
        "mp",
        scatter_dimension=0,
        tiled=True,
    ).astype(jnp.float32)
    every_grad = lax.all_gather(
        dest_grad.astype(jnp.bfloat16), ("segment", "dp"), axis=1, tiled=True
    ).astype(dest_grad.dtype)
    targets = lax.dynamic_slice_in_dim(frame_dest, group * owned, owned, 0)
    chooser = (jnp.arange(slots, dtype=jnp.int32)[None, :] == targets[:, None]).astype(jnp.float32)
    latent_grad = jnp.einsum("js,rse->rje", chooser, every_grad, precision=lax.Precision.HIGHEST)
    return (context, latent_grad)


def solution(mesh):
    in_specs = (
        P(("segment", "dp"), "mp", None),
        P(),
        P(),
        P(None, "mp"),
        P(None, None, "mp"),
        P(),
        P("segment", "dp", None, "mp"),
        P("segment", None),
        P("segment", "dp", "mp"),
        P("segment", "dp", None, "mp"),
        P("segment"),
        P("segment", "dp"),
        P(),
        P("segment", "dp", None, "mp"),
    )
    out_specs = (P("segment", "dp", None, "mp"), P("mp", ("segment", "dp"), None))
    return jax.shard_map(
        per_device, mesh=mesh, in_specs=in_specs, out_specs=out_specs, check_vma=False
    )
```

profile of v0, /device:TPU:1, one launch (start us, length us, event | category | flops | bytes accessed | tf_op | source)
XLA Modules:
  0.0 658.1 jit_solution(9813244482838572930)
XLA Ops:
  7.2 0.7 all-gather.11.cloned.1.call-update
  8.0 0.9 convert_reduce_fusion.3
  8.8 1.1 convert_reduce_fusion.2
  9.9 1.2 fusion.108
  11.1 1.3 fusion.99
  12.4 1.3 convolution_convert_fusion.3
  14.1 52.8 %all-gather.11.cloned.1.call-done = bf16[8,128,1536]{2,1,0:T(8,128)(2,1)} async-done(((bf16[8,8,1536]{2,1,0:T(8,128)(2,1)}), bf16[8,128,1536]{2,1,0:T(8,128)(2,1)}) %all-gather.11.cloned.1.call-update) | async-done | bytes 3145744 | tf_op jit(solution)/shard_map/all_gather | solution.py:91
  66.9 2.5 convert_reduce_fusion.1
  69.5 2.8 fusion.15
  72.3 1.5 fusion.93
  74.4 1.7 fusion.43
  76.2 2.0 copy.37
  78.3 0.8 dynamic-slice_convert_fusion
  79.0 75.6 %reduce-scatter.3.cloned.1.call-done = bf16[4,8,1536]{2,1,0:T(8,128)(2,1)} async-done(((bf16[64,8,1536]{2,1,0:T(8,128)(2,1)}), bf16[4,8,1536]{2,1,0:T(8,128)(2,1)}) %reduce-scatter.3.cloned.1.call-update) | async-done | bytes 98320 | tf_op jit(solution)/shard_map/reduce_scatter | solution.py:125
  154.6 1.0 fusion.118
  155.6 1.1 multiply_reduce_fusion
  156.7 1.0 multiply_convert_fusion
  157.7 0.7 copy.38
  158.4 2.1 copy.40
  160.6 38.4 %all-gather.13.cloned.1.call-done = bf16[4,128,1536]{2,0,1:T(4,128)(2,1)} async-done(((bf16[4,8,1536]{2,0,1:T(4,128)(2,1)}), bf16[4,128,1536]{2,0,1:T(4,128)(2,1)}) %all-gather.13.cloned.1.call-update) | async-done | bytes 1572880 | tf_op jit(solution)/shard_map/all_gather | solution.py:137
  199.0 2.4 fusion.49
  201.5 0.5 all-gather.21.cloned.1.call-update
  202.1 0.7 all-gather.23.cloned.1.call-update
  203.8 1.7 copy.46
  206.3 34.1 %all-gather.19.cloned.1.call-done = bf16[1,1536,2,512]{3,1,2,0:T(8,128)(2,1)} async-done(((bf16[1,384,2,512]{3,1,2,0:T(8,128)(2,1)}), bf16[1,1536,2,512]{3,1,2,0:T(8,128)(2,1)}) %all-gather.19.cloned.1.call-update) | async-done | bytes 3145744 | tf_op jit(solution)/shard_map/all_gather | solution.py:162
  240.4 50.8 %all-gather.15.cloned.1.call-done = bf16[64,8,1536]{2,1,0:T(8,128)(2,1)} async-done(((bf16[4,8,1536]{2,1,0:T(8,128)(2,1)}), bf16[64,8,1536]{2,1,0:T(8,128)(2,1)}) %all-gather.15.cloned.1.call-update) | async-done | bytes 1572880 | tf_op jit(solution)/shard_map/all_gather | solution.py:144
  291.2 4.1 fusion.69
  295.3 0.6 copy.41
  295.9 0.5 reshape.414
  296.4 0.4 fusion.148
  297.1 100.5 %all-gather.21.cloned.1.call-done = bf16[1,1,768,8192]{3,2,1,0:T(8,128)(2,1)} async-done(((bf16[1,1,768,512]{3,2,1,0:T(8,128)(2,1)}), bf16[1,1,768,8192]{3,2,1,0:T(8,128)(2,1)}) %all-gather.21.cloned.1.call-update) | async-done | bytes 12582928 | tf_op jit(solution)/shard_map/all_gather | solution.py:145
  397.7 6.4 convert_reduce_fusion
  404.0 8.0 %fusion.3 = f32[768]{0:T(1024)S(1)} fusion(bf16[1,1,768,8192]{3,2,1,0:T(8,128)(2,1)} %all-gather.21.cloned.1.call-done, f32[768]{0:T(1024)S(1)} %broadcast_multiply_fusion), kind=kLoop, calls=%fused_computation.5 | loop fusion | flops 25165056 | bytes 12589056 | tf_op jit(solution)/shard_map/reduce_sum | solution.py:17
  412.0 72.3 %all-gather.23.cloned.1.call-done = bf16[1,8192,512]{2,1,0:T(8,128)(2,1)} async-done(((bf16[1,2048,512]{2,1,0:T(8,128)(2,1)}), bf16[1,8192,512]{2,1,0:T(8,128)(2,1)}) %all-gather.23.cloned.1.call-update) | async-done | bytes 8388624 | tf_op jit(solution)/shard_map/all_gather | solution.py:158
  484.3 17.6 %fusion.64 = bf16[768,512]{0,1:T(8,128)(2,1)S(1)} fusion(bf16[1,8192,512]{2,1,0:T(8,128)(2,1)} %all-gather.23.cloned.1.call-done, bf16[1,1,768,8192]{3,2,1,0:T(8,128)(2,1)} %all-gather.21.cloned.1.call-done, f32[8192]{0:T(1024)S(1)} %bitcast.222, f32[768]{0:T(1024)S(1)} %add_rsqrt_fusion, f32[768]{0:T(1024)S(1)} %broadcast_multiply_fusion), kind=kOutput, calls=%fused_computation.65 | convolution fusion | flops 6474301440 | bytes 21796864 | tf_op jit(solution)/shard_map/dot_general | solution.py:156
  501.8 1.1 fusion.24
  502.9 1.4 fusion.25
  504.4 1.7 fusion.90
  506.2 2.8 fusion.53
  508.9 7.0 %fusion.85 = bf16[1,512,1,4,128]{1,4,3,2,0:T(8,128)(2,1)} fusion(bf16[768,4,128]{0,2,1:T(8,128)(2,1)S(1)} %bitcast.217, f32[4,768,512]{1,2,0:T(8,128)} %copy-done.2, f32[4,768]{1,0:T(4,128)S(1)} %negate_bitcast_fusion, f32[4,768]{1,0:T(4,128)S(1)} %get-tuple-element.21, pred[512]{0:T(512)(128)(4,1)S(1)} %broadcast_in_dim.37, ...), kind=kOutput, calls=%fused_computation.70 | convolution fusion | flops 820117504 | bytes 9736704 | tf_op jit(solution)/shard_map/transpose(jvp(vmap(rag,lag->arl)))/dot_general | solution.py:22
  516.0 2.1 pad_add_fusion
  518.1 2.8 reshape.439
  520.9 3.4 copy.54
  524.2 5.3 fusion.44
  529.6 77.0 %reduce-scatter.5.cloned.1.call-done = bf16[4,8,1536]{2,1,0:T(8,128)(2,1)} async-done(((bf16[64,8,1536]{2,1,0:T(8,128)(2,1)}), bf16[4,8,1536]{2,1,0:T(8,128)(2,1)}) %reduce-scatter.5.cloned.1.call-update) | async-done | bytes 98320 | tf_op jit(solution)/shard_map/reduce_scatter | solution.py:178
  606.7 1.2 copy.55
  607.9 41.2 %all-gather.17.cloned.1.call-done = bf16[4,128,1536]{2,1,0:T(8,128)(2,1)} async-done(((bf16[4,8,1536]{2,1,0:T(8,128)(2,1)}), bf16[4,128,1536]{2,1,0:T(8,128)(2,1)}) %all-gather.17.cloned.1.call-update) | async-done | bytes 1572880 | tf_op jit(solution)/shard_map/all_gather | solution.py:186
  649.1 2.5 convolution_bitcast_fusion.1
  (58 shorter events, 2.3 us)
Async XLA Ops:
  7.2 3.9 copy-start
  7.2 59.8 %all-gather.11.cloned.1.call-start = ((), (), s32[]{:S(2)}) async-start(), calls=%async_computation.2 | async-start | bytes 3342336 | tf_op jit(solution)/shard_map/all_gather | solution.py:91
  7.9 146.7 %reduce-scatter.3.cloned.1.call-start = ((), (), s32[]{:S(2)}) async-start(), calls=%async_computation.3 | async-start | bytes 1671168 | tf_op jit(solution)/shard_map/reduce_scatter | solution.py:125
  66.9 5.4 copy-start.3
  73.8 125.2 %copy-start.8 = (s32[128]{0:T(128)S(1)}, s32[128]{0:T(128)}, u32[]{:S(2)}) copy-start(s32[128]{0:T(128)} %param.26) | copy-start | bytes 1540
  76.2 127.4 %copy-start.5 = (bf16[1,1,768,512]{3,2,1,0:T(8,128)(2,1)S(1)}, bf16[1,1,768,512]{3,2,1,0:T(8,128)(2,1)}, u32[]{:S(2)}) copy-start(bf16[1,1,768,512]{3,2,1,0:T(8,128)(2,1)} %param.27) | copy-start | bytes 2359300
  78.2 120.8 %all-gather.13.cloned.1.call-start = ((), (), s32[]{:S(2)}) async-start(), calls=%async_computation.4 | async-start | bytes 1671168 | tf_op jit(solution)/shard_map/all_gather | solution.py:137
  158.4 47.9 %copy-start.7 = (bf16[1,8192]{1,0:T(2,128)(2,1)S(1)}, bf16[1,8192]{1,0:T(2,128)(2,1)}, u32[]{:S(2)}) copy-start(bf16[1,8192]{1,0:T(2,128)(2,1)} %param.21) | copy-start | bytes 49156
  158.4 82.0 %all-gather.19.cloned.1.call-start = ((), (), s32[]{:S(2)}) async-start(), calls=%async_computation.8 | async-start | bytes 3932160 | tf_op jit(solution)/shard_map/all_gather | solution.py:162
  160.6 130.6 %all-gather.15.cloned.1.call-start = ((), (), s32[]{:S(2)}) async-start(), calls=%async_computation.5 | async-start | bytes 1671168 | tf_op jit(solution)/shard_map/all_gather | solution.py:144
  201.5 196.2 %all-gather.21.cloned.1.call-start = ((), (), s32[]{:S(2)}) async-start(), calls=%async_computation.9 | async-start | bytes 13369344 | tf_op jit(solution)/shard_map/all_gather | solution.py:145
  202.1 282.2 %all-gather.23.cloned.1.call-start = ((), (), s32[]{:S(2)}) async-start(), calls=%async_computation.10 | async-start | bytes 10485760 | tf_op jit(solution)/shard_map/all_gather | solution.py:158
  202.8 403.8 %reduce-scatter.5.cloned.1.call-start = ((), (), s32[]{:S(2)}) async-start(), calls=%async_computation.6 | async-start | bytes 1671168 | tf_op jit(solution)/shard_map/reduce_scatter | solution.py:178
  501.8 2.6 copy-start.4
  502.9 3.2 copy-start.2
  524.2 82.5 %copy-start.6 = (bf16[1,768,4,128]{1,3,2,0:T(8,128)(2,1)S(1)}, bf16[1,768,4,128]{1,3,2,0:T(8,128)(2,1)}, u32[]{:S(2)}) copy-start(bf16[1,768,4,128]{1,3,2,0:T(8,128)(2,1)} %get-tuple-element.14) | copy-start | bytes 2359300
  524.2 127.3 %copy-start.1 = (bf16[1536,2,96]{0,2,1:T(8,128)(2,1)S(1)}, bf16[1536,2,96]{0,2,1:T(8,128)(2,1)}, u32[]{:S(2)}) copy-start(bf16[1536,2,96]{0,2,1:T(8,128)(2,1)} %param.18) | copy-start | bytes 1769476
  529.6 119.5 %all-gather.17.cloned.1.call-start = ((), (), s32[]{:S(2)}) async-start(), calls=%async_computation.7 | async-start | bytes 1671168 | tf_op jit(solution)/shard_map/all_gather | solution.py:186
Sparse Core Ops, SparseCore 0:
  10.4 56.4 all-gather.10
  78.3 76.1 reduce-scatter.2
  158.5 40.4 all-gather.12
  201.3 39.1 all-gather.18
  243.3 47.8 all-gather.14
  293.5 104.1 all-gather.20
  399.5 84.7 all-gather.22
  529.7 76.8 reduce-scatter.4
  608.5 40.5 all-gather.16
where the time goes:
time: 659 us; the launch traced here: 658 us
  waiting for transfers between devices  545 us (83%)
  matrix products  50.9 us (8%)
  other arithmetic  30.7 us (5%)
  local copies, waits for them, and re-layouts  15.8 us (2%)
  between operations  15.5 us (2%)
    all_gather x1, waiting for transfers between devices, per_device(): whole_text = lax.all_gather(text[0], 'mp', axis=2, tiled=True)  101 us
    reduce_scatter x1, waiting for transfers between devices, per_device(): lax.psum_scatter(jnp.einsum('jlkc,ekc->lje', part, full_kv, preferred_ele...  77 us
    reduce_scatter x1, waiting for transfers between devices, per_device(): lax.psum_scatter(jnp.einsum('fhlr,hre->lfe', part, out_heads, preferred_e...  75.6 us
    all_gather x1, waiting for transfers between devices, per_device(): lax.all_gather(w_query[0], 'dp', axis=0, tiled=True)  72.3 us
    all_gather x1, waiting for transfers between devices, per_device(): piece = lax.all_gather(frames, 'mp', axis=1, tiled=True)  52.8 us
    all_gather x1, waiting for transfers between devices, per_device(): dest = lax.all_gather(mine, 'mp', axis=0, tiled=True)  50.8 us
    all_gather x1, waiting for transfers between devices, per_device(): lax.all_gather(dest_grad.astype(jnp.bfloat16), ('segment', 'dp'), axis=1,...  41.2 us
    all_gather x1, waiting for transfers between devices, per_device(): gathered = lax.all_gather(latents, ('segment', 'dp'), axis=1, tiled=True)  38.4 us
  transfers between devices with their start and end apart: 9, of which 9 were waited for; matrix products, arithmetic and copies ran while one was open for 5% of the time, Pallas kernels for 0%

commit v1 on v0

--- a/solution.py
+++ b/solution.py
@@ -9,6 +9,12 @@
 RESAMPLE_HEAD_DIM = 96
 LAT = 64
 FMAX = 8
+
+
+def laid_out(blocks, dim):
+    lengths = list(blocks.shape[1:])
+    lengths[dim] *= blocks.shape[0]
+    return jnp.moveaxis(blocks, 0, dim).reshape(lengths)
 
 
 def layer_norm(inputs, gain_row):
@@ -141,7 +147,6 @@
     mine = jnp.einsum("js,rse->rje", picker, gathered, preferred_element_type=jnp.float32).astype(
         jnp.bfloat16
     )
-    dest = lax.all_gather(mine, "mp", axis=0, tiled=True)
     whole_text = lax.all_gather(text[0], "mp", axis=2, tiled=True)
     seq_local = whole_text.shape[0]
     txt_len = whole_text.shape[1]
@@ -160,7 +165,26 @@
     )
     query_matrix = query_sum.astype(jnp.bfloat16).reshape(seq_local, txt_len, head_local, HD)
     full_kv = lax.all_gather(w_kv[0], "dp", axis=0, tiled=True)
-    pair_sum = jnp.einsum("lje,ekc->jlkc", dest, full_kv, preferred_element_type=jnp.float32)
+    peers, position, span = (lax.axis_size("mp"), lax.axis_index("mp"), mine.shape[0])
+    right = [(i, (i + 1) % peers) for i in range(peers)]
+    left = [(i, (i - 1) % peers) for i in range(peers)]
+    middle = peers // 2
+    blocks = {}
+    from_left = from_right = mine
+    for hop in range(middle + 1):
+        next_left = lax.ppermute(from_left, "mp", right) if hop < middle else None
+        next_right = lax.ppermute(from_right, "mp", left) if hop < peers - middle - 1 else None
+        blocks[-hop] = jnp.einsum(
+            "lje,ekc->jlkc", from_left, full_kv, preferred_element_type=jnp.float32
+        )
+        if 0 < hop < peers - middle:
+            blocks[hop] = jnp.einsum(
+                "lje,ekc->jlkc", from_right, full_kv, preferred_element_type=jnp.float32
+            )
+        from_left, from_right = (next_left, next_right)
+    blocks = jnp.stack([blocks[k] for k in sorted(blocks)])
+    blocks = blocks[(jnp.arange(peers) - position + middle) % peers]
+    pair_sum = laid_out(blocks, 1)
     pair_list = pair_sum.astype(jnp.bfloat16).reshape(seq_local, FMAX * LAT, 2, head_local, HD)
     live = jnp.repeat(
         jnp.arange(FMAX, dtype=jnp.int32)[None, :] < frame_counts[0][:, None], LAT, axis=1

time: 659 us -> 618 us (0.938); the launches traced: 658 us -> 608 us
  waiting for transfers between devices: 545 us -> 451 us
  starting transfers between devices: 0.36 us -> 36.6 us
  matrix products: 50.9 us -> 57.8 us
    all_gather x1 -> x0, waiting for transfers between devices: 50.8 us -> none  [per_device(): dest = lax.all_gather(mine, 'mp', axis=0, tiled=True)]
    ppermute x0 -> x15, starting transfers between devices: none -> 36.2 us  [the longest x7 34.8 us: per_device(): lax.ppermute(from_right, 'mp', left)]
    all_gather x1, waiting for transfers between devices: 34.1 us -> 0.01 us  [per_device(): full_kv = lax.all_gather(w_kv[0], 'dp', axis=0, tiled=True)]
    all_gather x1, waiting for transfers between devices: 101 us -> 75.2 us  [per_device(): whole_text = lax.all_gather(text[0], 'mp', axis=2, tiled=True)]
    ppermute x0 -> x15, waiting for transfers between devices: none -> 17.2 us  [the longest x8 12 us: per_device(): next_left = lax.ppermute(from_left, 'mp', right) if hop < middle else None]
    dot_general x1 -> x16, matrix products: 4.14 us -> 11.6 us  [the longest x9 7.5 us: per_device(): jnp.einsum('lje,ekc->jlkc', from_left, full_kv, preferred_element_type=jn...]
  transfers between devices with their start and end apart: 9 -> 23, of which waited for: 9 -> 15; matrix products, arithmetic and copies ran while one was open for 5% -> 7% of each run, Pallas kernels for 0% -> 0%
where the time goes in v1:
time: 618 us; the launch traced here: 608 us
  waiting for transfers between devices  451 us (73%)
  matrix products  57.8 us (9%)
  starting transfers between devices  36.6 us (6%)
  other arithmetic  28.9 us (5%)
  local copies, waits for them, and re-layouts  17.4 us (3%)
  between operations  16.3 us (3%)
    reduce_scatter x1, waiting for transfers between devices, per_device(): lax.psum_scatter(jnp.einsum('jlkc,ekc->lje', part, full_kv, preferred_ele...  77.1 us
    reduce_scatter x1, waiting for transfers between devices, per_device(): lax.psum_scatter(jnp.einsum('fhlr,hre->lfe', part, out_heads, preferred_e...  75.7 us
    all_gather x1, waiting for transfers between devices, per_device(): whole_text = lax.all_gather(text[0], 'mp', axis=2, tiled=True)  75.2 us
    all_gather x1, waiting for transfers between devices, per_device(): lax.all_gather(w_query[0], 'dp', axis=0, tiled=True)  72.1 us
    all_gather x1, waiting for transfers between devices, per_device(): piece = lax.all_gather(frames, 'mp', axis=1, tiled=True)  52.8 us
    all_gather x1, waiting for transfers between devices, per_device(): lax.all_gather(dest_grad.astype(jnp.bfloat16), ('segment', 'dp'), axis=1,...  41.1 us
    all_gather x1, waiting for transfers between devices, per_device(): gathered = lax.all_gather(latents, ('segment', 'dp'), axis=1, tiled=True)  38.4 us
    ppermute x7, starting transfers between devices, per_device(): lax.ppermute(from_right, 'mp', left)  34.8 us
  transfers between devices with their start and end apart: 23, of which 15 were waited for; matrix products, arithmetic and copies ran while one was open for 7% of the time, Pallas kernels for 0%

profile of v1, /device:TPU:1, one launch (start us, length us, event | category | flops | bytes accessed | tf_op | source)
XLA Modules:
  0.0 608.4 jit_solution(7218585905907355870)
XLA Ops:
  9.9 1.2 fusion.222
  11.1 1.3 fusion.213
  12.4 1.3 convolution_convert_fusion.3
  14.1 52.8 %all-gather.10.cloned.1.call-done = bf16[8,128,1536]{2,1,0:T(8,128)(2,1)} async-done(((bf16[8,8,1536]{2,1,0:T(8,128)(2,1)}), bf16[8,128,1536]{2,1,0:T(8,128)(2,1)}) %all-gather.10.cloned.1.call-update) | async-done | bytes 3145744 | tf_op jit(solution)/shard_map/all_gather | solution.py:97
  66.9 2.5 convert_reduce_fusion.1
  70.7 1.5 fusion.111
  72.8 1.7 fusion.73
  74.6 2.0 copy.39
  77.4 75.7 %reduce-scatter.3.cloned.1.call-done = bf16[4,8,1536]{2,1,0:T(8,128)(2,1)} async-done(((bf16[64,8,1536]{2,1,0:T(8,128)(2,1)}), bf16[4,8,1536]{2,1,0:T(8,128)(2,1)}) %reduce-scatter.3.cloned.1.call-update) | async-done | bytes 98320 | tf_op jit(solution)/shard_map/reduce_scatter | solution.py:131
  154.1 1.1 multiply_reduce_fusion
  159.2 38.4 %all-gather.12.cloned.1.call-done = bf16[4,128,1536]{2,0,1:T(4,128)(2,1)} async-done(((bf16[4,8,1536]{2,0,1:T(4,128)(2,1)}), bf16[4,128,1536]{2,0,1:T(4,128)(2,1)}) %all-gather.12.cloned.1.call-update) | async-done | bytes 1572880 | tf_op jit(solution)/shard_map/all_gather | solution.py:143
  197.6 1.7 convolution_convert_fusion.1
  199.3 1.3 collective-permute-start
  200.6 6.3 %collective-permute-done = bf16[4,8,1536]{2,1,0:T(8,128)(2,1)S(1)} collective-permute-done((bf16[4,8,1536]{2,1,0:T(8,128)(2,1)S(1)}, bf16[4,8,1536]{2,1,0:T(8,128)(2,1)S(1)}, u32[]{:S(2)}, u32[]{:S(2)}) %collective-permute-start) | collective-permute-done | bytes 98336 | tf_op jit(solution)/shard_map/ppermute | solution.py:175
  206.9 4.8 collective-permute-start.8
  211.7 2.0 collective-permute-done.1
  213.7 4.8 collective-permute-start.9
  218.5 2.0 collective-permute-done.2
  221.2 4.9 collective-permute-start.10
  226.0 1.2 collective-permute-done.3
  227.6 1.7 copy.48
  230.0 4.8 collective-permute-start.11
  235.1 1.4 collective-permute-done.11
  236.5 5.1 collective-permute-start.12
  241.7 1.6 collective-permute-done.12
  243.3 5.1 collective-permute-start.13
  248.4 2.2 collective-permute-done.13
  250.7 5.2 collective-permute-start.14
  256.4 2.8 fusion.120
  271.1 75.2 %all-gather.18.cloned.1.call-done = bf16[1,1,768,8192]{3,2,1,0:T(8,128)(2,1)} async-done(((bf16[1,1,768,512]{3,2,1,0:T(8,128)(2,1)}), bf16[1,1,768,8192]{3,2,1,0:T(8,128)(2,1)}) %all-gather.18.cloned.1.call-update) | async-done | bytes 12582928 | tf_op jit(solution)/shard_map/all_gather | solution.py:150
  346.3 6.4 %convert_reduce_fusion = f32[768]{0:T(1024)S(1)} fusion(bf16[1,1,768,8192]{3,2,1,0:T(8,128)(2,1)} %all-gather.18.cloned.1.call-done), kind=kLoop, calls=%fused_computation.1 | loop fusion | flops 12582144 | bytes 12585984 | tf_op jit(solution)/shard_map/reduce_sum | solution.py:22
  352.6 8.0 %fusion.3 = f32[768]{0:T(1024)S(1)} fusion(bf16[1,1,768,8192]{3,2,1,0:T(8,128)(2,1)} %all-gather.18.cloned.1.call-done, f32[768]{0:T(1024)S(1)} %broadcast_multiply_fusion), kind=kLoop, calls=%fused_computation.6 | loop fusion | flops 25165056 | bytes 12589056 | tf_op jit(solution)/shard_map/reduce_sum | solution.py:23
  360.6 72.1 %all-gather.20.cloned.1.call-done = bf16[1,8192,512]{2,1,0:T(8,128)(2,1)} async-done(((bf16[1,2048,512]{2,1,0:T(8,128)(2,1)}), bf16[1,8192,512]{2,1,0:T(8,128)(2,1)}) %all-gather.20.cloned.1.call-update) | async-done | bytes 8388624 | tf_op jit(solution)/shard_map/all_gather | solution.py:163
  432.7 17.6 %fusion.87 = bf16[768,512]{0,1:T(8,128)(2,1)S(1)} fusion(bf16[1,8192,512]{2,1,0:T(8,128)(2,1)} %all-gather.20.cloned.1.call-done, bf16[1,1,768,8192]{3,2,1,0:T(8,128)(2,1)} %all-gather.18.cloned.1.call-done, f32[8192]{0:T(1024)S(1)} %bitcast.479, f32[768]{0:T(1024)S(1)} %add_rsqrt_fusion, f32[768]{0:T(1024)S(1)} %broadcast_multiply_fusion), kind=kOutput, calls=%fused_computation.93 | convolution fusion | flops 6474301440 | bytes 21796864 | tf_op jit(solution)/shard_map/dot_general | solution.py:161
  450.3 1.1 fusion.24
  451.4 1.4 fusion.25
  452.9 1.1 copy-done.4
  454.0 1.7 fusion.108
  455.7 2.8 fusion.81
  458.5 7.0 %fusion.103 = bf16[1,512,1,4,128]{1,4,3,2,0:T(8,128)(2,1)} fusion(bf16[768,4,128]{0,2,1:T(8,128)(2,1)S(1)} %bitcast.474, f32[4,768,512]{1,2,0:T(8,128)} %copy-done.2, f32[4,768]{1,0:T(4,128)S(1)} %negate_bitcast_fusion, f32[4,768]{1,0:T(4,128)S(1)} %get-tuple-element.21, pred[512]{0:T(512)(128)(4,1)S(1)} %broadcast_in_dim.37, ...), kind=kOutput, calls=%fused_computation.97 | convolution fusion | flops 820117504 | bytes 9736704 | tf_op jit(solution)/shard_map/transpose(jvp(vmap(rag,lag->arl)))/dot_general | solution.py:28
  465.6 2.1 pad_add_fusion
  467.7 2.8 reshape.523
  470.5 3.4 copy.56
  473.8 5.3 fusion.74
  479.2 77.1 %reduce-scatter.5.cloned.1.call-done = bf16[4,8,1536]{2,1,0:T(8,128)(2,1)} async-done(((bf16[64,8,1536]{2,1,0:T(8,128)(2,1)}), bf16[4,8,1536]{2,1,0:T(8,128)(2,1)}) %reduce-scatter.5.cloned.1.call-update) | async-done | bytes 98320 | tf_op jit(solution)/shard_map/reduce_scatter | solution.py:202
  556.4 1.2 copy.57
  557.5 41.1 %all-gather.14.cloned.1.call-done = bf16[4,128,1536]{2,1,0:T(8,128)(2,1)} async-done(((bf16[4,8,1536]{2,1,0:T(8,128)(2,1)}), bf16[4,128,1536]{2,1,0:T(8,128)(2,1)}) %all-gather.14.cloned.1.call-update) | async-done | bytes 1572880 | tf_op jit(solution)/shard_map/all_gather | solution.py:210
  598.7 2.5 convolution_bitcast_fusion.1
  (107 shorter events, 23.8 us)
Async XLA Ops:
  7.2 3.9 copy-start
  7.2 59.8 %all-gather.10.cloned.1.call-start = ((), (), s32[]{:S(2)}) async-start(), calls=%async_computation.2 | async-start | bytes 3342336 | tf_op jit(solution)/shard_map/all_gather | solution.py:97
  7.9 145.2 %reduce-scatter.3.cloned.1.call-start = ((), (), s32[]{:S(2)}) async-start(), calls=%async_computation.3 | async-start | bytes 1671168 | tf_op jit(solution)/shard_map/reduce_scatter | solution.py:131
  66.9 2.8 copy-start.3
  74.6 82.4 %copy-start.6 = (bf16[1,384,2,512]{3,2,1,0:T(2,128)(2,1)S(1)}, bf16[1,384,2,512]{3,2,1,0:T(2,128)(2,1)}, u32[]{:S(2)}) copy-start(bf16[1,384,2,512]{3,2,1,0:T(2,128)(2,1)} %param.23) | copy-start | bytes 2359300
  76.6 121.0 %copy-start.10 = (s32[128]{0:T(128)S(1)}, s32[128]{0:T(128)}, u32[]{:S(2)}) copy-start(s32[128]{0:T(128)} %param.26) | copy-start | bytes 1540
  76.6 121.0 %all-gather.12.cloned.1.call-start = ((), (), s32[]{:S(2)}) async-start(), calls=%async_computation.4 | async-start | bytes 1671168 | tf_op jit(solution)/shard_map/all_gather | solution.py:143
  156.9 99.0 %all-gather.16.cloned.1.call-start = ((), (), s32[]{:S(2)}) async-start(), calls=%async_computation.7 | async-start | bytes 3932160 | tf_op jit(solution)/shard_map/all_gather | solution.py:167
  157.9 69.5 %copy-start.5 = (bf16[1,1,768,512]{3,2,1,0:T(8,128)(2,1)S(1)}, bf16[1,1,768,512]{3,2,1,0:T(8,128)(2,1)}, u32[]{:S(2)}) copy-start(bf16[1,1,768,512]{3,2,1,0:T(8,128)(2,1)} %param.27) | copy-start | bytes 2359300
  158.0 188.3 %all-gather.18.cloned.1.call-start = ((), (), s32[]{:S(2)}) async-start(), calls=%async_computation.8 | async-start | bytes 13369344 | tf_op jit(solution)/shard_map/all_gather | solution.py:150
  158.5 274.2 %all-gather.20.cloned.1.call-start = ((), (), s32[]{:S(2)}) async-start(), calls=%async_computation.9 | async-start | bytes 10485760 | tf_op jit(solution)/shard_map/all_gather | solution.py:163
  159.1 397.1 %reduce-scatter.5.cloned.1.call-start = ((), (), s32[]{:S(2)}) async-start(), calls=%async_computation.5 | async-start | bytes 1671168 | tf_op jit(solution)/shard_map/reduce_scatter | solution.py:202
  199.3 35.7 %copy-start.8 = (bf16[1,8192]{1,0:T(2,128)(2,1)S(1)}, bf16[1,8192]{1,0:T(2,128)(2,1)}, u32[]{:S(2)}) copy-start(bf16[1,8192]{1,0:T(2,128)(2,1)} %param.21) | copy-start | bytes 49156
  199.3 7.5 %collective-permute-start = (bf16[4,8,1536]{2,1,0:T(8,128)(2,1)S(1)}, bf16[4,8,1536]{2,1,0:T(8,128)(2,1)S(1)}, u32[]{:S(2)}, u32[]{:S(2)}) collective-permute-start(bf16[4,8,1536]{2,1,0:T(8,128)(2,1)S(1)} %bitcast.480), channel_id=1, source_target_pairs={{0,4},{4,8},{8,12},{12,16},{16,20},{20,24},{24,28},{28,32},{32,36}... | collective-permute-start | bytes 294920 | tf_op jit(solution)/shard_map/ppermute | solution.py:175
  206.9 6.8 %collective-permute-start.1 = (bf16[4,8,1536]{2,1,0:T(8,128)(2,1)S(1)}, bf16[4,8,1536]{2,1,0:T(8,128)(2,1)S(1)}, u32[]{:S(2)}, u32[]{:S(2)}) collective-permute-start(bf16[4,8,1536]{2,1,0:T(8,128)(2,1)S(1)} %collective-permute-done), channel_id=1, source_target_pairs={{0,4},{4,8},{8,12},{12,16},{16,20},{20,24},{24,28},{28,32},{32,36}... | collective-permute-start | bytes 294920 | tf_op jit(solution)/shard_map/ppermute | solution.py:175
  206.9 6.8 %collective-permute-start.8 = (bf16[4,8,1536]{2,1,0:T(8,128)(2,1)S(1)}, bf16[4,8,1536]{2,1,0:T(8,128)(2,1)S(1)}, u32[]{:S(2)}, u32[]{:S(2)}) collective-permute-start(bf16[4,8,1536]{2,1,0:T(8,128)(2,1)S(1)} %bitcast.481), channel_id=1, source_target_pairs={{0,60},{4,0},{8,4},{12,8},{16,12},{20,16},{24,20},{28,24},{32,28},... | collective-permute-start | bytes 294920 | tf_op jit(solution)/shard_map/ppermute | solution.py:176
  213.7 6.8 %collective-permute-start.2 = (bf16[4,8,1536]{2,1,0:T(8,128)(2,1)S(1)}, bf16[4,8,1536]{2,1,0:T(8,128)(2,1)S(1)}, u32[]{:S(2)}, u32[]{:S(2)}) collective-permute-start(bf16[4,8,1536]{2,1,0:T(8,128)(2,1)S(1)} %collective-permute-done.1), channel_id=1, source_target_pairs={{0,4},{4,8},{8,12},{12,16},{16,20},{20,24},{24,28},{28,32},{32,36}... | collective-permute-start | bytes 294920 | tf_op jit(solution)/shard_map/ppermute | solution.py:175
  213.7 7.5 %collective-permute-start.9 = (bf16[4,8,1536]{2,1,0:T(8,128)(2,1)S(1)}, bf16[4,8,1536]{2,1,0:T(8,128)(2,1)S(1)}, u32[]{:S(2)}, u32[]{:S(2)}) collective-permute-start(bf16[4,8,1536]{2,1,0:T(8,128)(2,1)S(1)} %collective-permute-done.8), channel_id=1, source_target_pairs={{0,60},{4,0},{8,4},{12,8},{16,12},{20,16},{24,20},{28,24},{32,28},... | collective-permute-start | bytes 294920 | tf_op jit(solution)/shard_map/ppermute | solution.py:176
  220.5 6.8 %collective-permute-start.3 = (bf16[4,8,1536]{2,1,0:T(8,128)(2,1)S(1)}, bf16[4,8,1536]{2,1,0:T(8,128)(2,1)S(1)}, u32[]{:S(2)}, u32[]{:S(2)}) collective-permute-start(bf16[4,8,1536]{2,1,0:T(8,128)(2,1)S(1)} %collective-permute-done.2), channel_id=1, source_target_pairs={{0,4},{4,8},{8,12},{12,16},{16,20},{20,24},{24,28},{28,32},{32,36}... | collective-permute-start | bytes 294920 | tf_op jit(solution)/shard_map/ppermute | solution.py:175
  221.2 8.8 %collective-permute-start.10 = (bf16[4,8,1536]{2,1,0:T(8,128)(2,1)S(1)}, bf16[4,8,1536]{2,1,0:T(8,128)(2,1)S(1)}, u32[]{:S(2)}, u32[]{:S(2)}) collective-permute-start(bf16[4,8,1536]{2,1,0:T(8,128)(2,1)S(1)} %collective-permute-done.9), channel_id=1, source_target_pairs={{0,60},{4,0},{8,4},{12,8},{16,12},{20,16},{24,20},{28,24},{32,28},... | collective-permute-start | bytes 294920 | tf_op jit(solution)/shard_map/ppermute | solution.py:176
  227.2 7.6 %collective-permute-start.4 = (bf16[4,8,1536]{2,1,0:T(8,128)(2,1)S(1)}, bf16[4,8,1536]{2,1,0:T(8,128)(2,1)S(1)}, u32[]{:S(2)}, u32[]{:S(2)}) collective-permute-start(bf16[4,8,1536]{2,1,0:T(8,128)(2,1)S(1)} %collective-permute-done.3), channel_id=1, source_target_pairs={{0,4},{4,8},{8,12},{12,16},{16,20},{20,24},{24,28},{28,32},{32,36}... | collective-permute-start | bytes 294920 | tf_op jit(solution)/shard_map/ppermute | solution.py:175
  230.0 6.5 %collective-permute-start.11 = (bf16[4,8,1536]{2,1,0:T(8,128)(2,1)S(1)}, bf16[4,8,1536]{2,1,0:T(8,128)(2,1)S(1)}, u32[]{:S(2)}, u32[]{:S(2)}) collective-permute-start(bf16[4,8,1536]{2,1,0:T(8,128)(2,1)S(1)} %collective-permute-done.10), channel_id=1, source_target_pairs={{0,60},{4,0},{8,4},{12,8},{16,12},{20,16},{24,20},{28,24},{32,28},... | collective-permute-start | bytes 294920 | tf_op jit(solution)/shard_map/ppermute | solution.py:176
  234.9 6.8 %collective-permute-start.5 = (bf16[4,8,1536]{2,1,0:T(8,128)(2,1)S(1)}, bf16[4,8,1536]{2,1,0:T(8,128)(2,1)S(1)}, u32[]{:S(2)}, u32[]{:S(2)}) collective-permute-start(bf16[4,8,1536]{2,1,0:T(8,128)(2,1)S(1)} %collective-permute-done.4), channel_id=1, source_target_pairs={{0,4},{4,8},{8,12},{12,16},{16,20},{20,24},{24,28},{28,32},{32,36}... | collective-permute-start | bytes 294920 | tf_op jit(solution)/shard_map/ppermute | solution.py:175
  236.5 6.8 %collective-permute-start.12 = (bf16[4,8,1536]{2,1,0:T(8,128)(2,1)S(1)}, bf16[4,8,1536]{2,1,0:T(8,128)(2,1)S(1)}, u32[]{:S(2)}, u32[]{:S(2)}) collective-permute-start(bf16[4,8,1536]{2,1,0:T(8,128)(2,1)S(1)} %collective-permute-done.11), channel_id=1, source_target_pairs={{0,60},{4,0},{8,4},{12,8},{16,12},{20,16},{24,20},{28,24},{32,28},... | collective-permute-start | bytes 294920 | tf_op jit(solution)/shard_map/ppermute | solution.py:176
  241.6 6.8 %collective-permute-start.6 = (bf16[4,8,1536]{2,1,0:T(8,128)(2,1)S(1)}, bf16[4,8,1536]{2,1,0:T(8,128)(2,1)S(1)}, u32[]{:S(2)}, u32[]{:S(2)}) collective-permute-start(bf16[4,8,1536]{2,1,0:T(8,128)(2,1)S(1)} %collective-permute-done.5), channel_id=1, source_target_pairs={{0,4},{4,8},{8,12},{12,16},{16,20},{20,24},{24,28},{28,32},{32,36}... | collective-permute-start | bytes 294920 | tf_op jit(solution)/shard_map/ppermute | solution.py:175
  243.3 7.4 %collective-permute-start.13 = (bf16[4,8,1536]{2,1,0:T(8,128)(2,1)S(1)}, bf16[4,8,1536]{2,1,0:T(8,128)(2,1)S(1)}, u32[]{:S(2)}, u32[]{:S(2)}) collective-permute-start(bf16[4,8,1536]{2,1,0:T(8,128)(2,1)S(1)} %collective-permute-done.12), channel_id=1, source_target_pairs={{0,60},{4,0},{8,4},{12,8},{16,12},{20,16},{24,20},{28,24},{32,28},... | collective-permute-start | bytes 294920 | tf_op jit(solution)/shard_map/ppermute | solution.py:176
  248.4 7.9 %collective-permute-start.7 = (bf16[4,8,1536]{2,1,0:T(8,128)(2,1)S(1)}, bf16[4,8,1536]{2,1,0:T(8,128)(2,1)S(1)}, u32[]{:S(2)}, u32[]{:S(2)}) collective-permute-start(bf16[4,8,1536]{2,1,0:T(8,128)(2,1)S(1)} %collective-permute-done.6), channel_id=1, source_target_pairs={{0,4},{4,8},{8,12},{12,16},{16,20},{20,24},{24,28},{28,32},{32,36}... | collective-permute-start | bytes 294920 | tf_op jit(solution)/shard_map/ppermute | solution.py:175
  250.7 16.8 %collective-permute-start.14 = (bf16[4,8,1536]{2,1,0:T(8,128)(2,1)S(1)}, bf16[4,8,1536]{2,1,0:T(8,128)(2,1)S(1)}, u32[]{:S(2)}, u32[]{:S(2)}) collective-permute-start(bf16[4,8,1536]{2,1,0:T(8,128)(2,1)S(1)} %collective-permute-done.13), channel_id=1, source_target_pairs={{0,60},{4,0},{8,4},{12,8},{16,12},{20,16},{24,20},{28,24},{32,28},... | collective-permute-start | bytes 294920 | tf_op jit(solution)/shard_map/ppermute | solution.py:176
  255.9 3.3 copy-start.9
  451.4 4.3 copy-start.2
  451.4 2.6 copy-start.4
  473.8 82.6 %copy-start.7 = (bf16[1,768,4,128]{1,3,2,0:T(8,128)(2,1)S(1)}, bf16[1,768,4,128]{1,3,2,0:T(8,128)(2,1)}, u32[]{:S(2)}) copy-start(bf16[1,768,4,128]{1,3,2,0:T(8,128)(2,1)} %get-tuple-element.14) | copy-start | bytes 2359300
  473.8 127.3 %copy-start.1 = (bf16[1536,2,96]{0,2,1:T(8,128)(2,1)S(1)}, bf16[1536,2,96]{0,2,1:T(8,128)(2,1)}, u32[]{:S(2)}) copy-start(bf16[1536,2,96]{0,2,1:T(8,128)(2,1)} %param.18) | copy-start | bytes 1769476
  479.1 119.5 %all-gather.14.cloned.1.call-start = ((), (), s32[]{:S(2)}) async-start(), calls=%async_computation.6 | async-start | bytes 1671168 | tf_op jit(solution)/shard_map/all_gather | solution.py:210
Sparse Core Ops, SparseCore 0:
  10.4 56.4 all-gather.9
  76.7 76.3 reduce-scatter.2
  157.0 40.5 all-gather.11
  199.8 39.2 all-gather.15
  241.4 104.7 all-gather.17
  347.9 84.7 all-gather.19
  479.3 76.9 reduce-scatter.4
  558.1 40.5 all-gather.13
